TPU v7x, 32 devices: a whole 2x2x4 slice. The times are simulated.
32 devices in a mesh: dp: 16 (over z, y, core), ctx: 2 (over x).
Axes of the slice: x: 2, y: 2, z: 4, core: 2. Of those that a mesh axis runs over, the one named last changes fastest.
Arguments:
- tokens: bfloat16 [16, 1024, 768], P('dp', 'ctx'), may hold values from -6 to 6
- w_query: bfloat16 [768, 768], P('dp'), may hold values from -0.21875 to 0.21875
- w_key: bfloat16 [768, 768], P('dp'), may hold values from -0.21875 to 0.21875
- w_value: bfloat16 [768, 768], P('dp'), may hold values from -0.21875 to 0.21875
- w_out: bfloat16 [768, 768], P('dp')
- w_up: bfloat16 [768, 3072], P('dp'), may hold values from -0.21875 to 0.21875
- w_down: bfloat16 [3072, 768], P('dp'), may hold values from -0.109375 to 0.109375
- gain_attn: bfloat16 [768], P('dp'), may hold values from 0.5 to 1.5
- gain_ffn: bfloat16 [768], P('dp'), may hold values from 0.5 to 1.5
- teacher: bfloat16 [16, 1024, 768], P('dp', 'ctx'), may hold values from -6 to 6
- seq_lengths: int32 [16], P('dp'), may hold values from 1 to 1024, 10240 in all
- tok_perm: int32 [16, 1024], P('dp'), may hold values from 0 to 1023, as said below
- valid_count: int32 [1], replicated, may hold values from 512 to 16384
Outputs:
- activations: bfloat16 [16, 1024, 768], P('dp', 'ctx')
- loss: float32 [1], replicated
- token_grad: float32 [16, 1024, 768], P('dp', 'ctx')
- w_query_grad: float32 [768, 768], P('dp')
- w_key_grad: float32 [768, 768], P('dp')
- w_value_grad: float32 [768, 768], P('dp')
- w_out_grad: float32 [768, 768], P('dp')
- w_up_grad: float32 [768, 3072], P('dp')
- w_down_grad: float32 [3072, 768], P('dp')
- gain_attn_grad: float32 [768], P('dp')
- gain_ffn_grad: float32 [768], P('dp')
Inputs may be any that keep to these rules, and one draw needn't show every extreme that they name: `tok_perm`: each row is a permutation of 0 to 1023. With G = 2 and B = 512 // G, dealt row c * 512 + t * B + j (0 <= j < B) holds a position from t * 512 to (t + 1) * 512 - 1. `seq_lengths`: the longest sequence has exactly 1024 valid tokens; all together have 5 * 1024 * 2.
All inputs are finite; a program needn't handle non-finite values. No bound on the sum of `seq_lengths` on one device may be relied on, other than what follows from the above.
Results may differ from a plain program's by a relative error of at most 0.023.
Values may be sent and summed in bfloat16 or wider, within the bound.
A program may use at most 192 MiB of HBM per device.

v0:
```python
import functools
import math

import jax
import jax.numpy as jnp
from jax import lax
from jax.experimental import pallas as pl
from jax.experimental.pallas import tpu as pltpu
from jax.sharding import PartitionSpec as P

HEAD_DIM = 64


EPSILON = 1e-06
SCORE_SCALE = 0.125
MASKED = -1e30
MESH = pl.DeviceIdType.MESH
MIB = 1024 * 1024


GATHER_SPLIT = (1, 3, 5, 6, 7, 8, 9)
REDUCE_SPLIT = (1, 2, 7, 8, 9, 11)
EARLY = 4
FORWARD = ((0, 1, 2, 3, 4, 5, 6, 7, 8, 9, 10), (), (0, 1, 0, 0, 2, 2, 3, 2, 1, 3, 4, 1, 5, 1), (), (3, 4, 6), (3,), (4, 5, 7), (6,), (8,), (5,), (5, 7), (), (), (6, 9), (), (6,), (), (8,), (), (), (7, 7), (10,), (9, 8, 8), (), (9, 10, 9), (), (10,), ())
BACKWARD = ((0, 1), (0, 2), (3,), (1, 4), (2, 5), (3, 0, 6), (4, 5, 1, 0, 6, 7), (2, 7, 4), (), (3, 0, 1, 5, 8), (), (8, 4, 6), (2,), (), (5,), (7,), (1, 9), (3, 6, 10), (2, 8, 4, 9, 5, 10, 11), (2, 6, 7, 8, 11, 12), (3, 9, 12), (), (11, 8, 10, 7, 9, 3, 10, 11, 12, 8, 9, 11, 12, 10, 9, 10, 12, 12))


def gelu_exact(values):
    return 0.5 * values * (1.0 + lax.erf(values * 0.7071067811865476))


def norm_forward(hidden, gain_row):
    center = hidden - jnp.mean(hidden, axis=-1, keepdims=True)
    inverse = lax.rsqrt(jnp.mean(center * center, axis=-1, keepdims=True) + EPSILON)
    normal = center * inverse
    return (normal * gain_row, normal, inverse)


def norm_backward(grad_norm, gain_row, normal, inverse):
    scaled = grad_norm * gain_row
    grad_input = inverse * (
        scaled
        - jnp.mean(scaled, axis=-1, keepdims=True)
        - normal * jnp.mean(scaled * normal, axis=-1, keepdims=True)
    )
    return (grad_input, jnp.sum(grad_norm * normal, axis=0))


def row_product(left_mat, right_mat):
    return lax.dot_general(
        left_mat, right_mat, (((0,), (0,)), ((), ())), preferred_element_type=jnp.float32
    )


def by_transpose(left_mat, right_mat):
    return lax.dot_general(
        left_mat, right_mat, (((1,), (1,)), ((), ())), preferred_element_type=jnp.float32
    )


def shards(
    tokens,
    w_query,
    w_key,
    w_value,
    w_out,
    w_up,
    w_down,
    gain_attn,
    gain_ffn,
    teacher,
    seq_lengths,
    tok_perm,
    valid_count,
):
    ctx_count = lax.axis_size("ctx")
    ctx_rank = lax.axis_index("ctx")
    dp_count = lax.axis_size("dp")
    layer_in = tokens[0]
    span_rows, model_width = layer_in.shape
    head_count = model_width // HEAD_DIM
    dealt_order = tok_perm[0]
    seq_len = dealt_order.shape[0]
    length = seq_lengths[0]
    keep_all = dealt_order < length
    per_peer = span_rows // ctx_count
    query_weight, key_weight, value_weight, out_weight, gain_first = (
        lax.all_gather(w_query, "dp", axis=0, tiled=True),
        lax.all_gather(w_key, "dp", axis=0, tiled=True),
        lax.all_gather(w_value, "dp", axis=0, tiled=True),
        lax.all_gather(w_out, "dp", axis=0, tiled=True),
        lax.all_gather(gain_attn, "dp", axis=0, tiled=True),
    )
    up_weight, down_weight, gain_second = (
        lax.all_gather(w_up, "dp", axis=0, tiled=True),
        lax.all_gather(w_down, "dp", axis=0, tiled=True),
        lax.all_gather(gain_ffn, "dp", axis=0, tiled=True),
    )
    queries = jnp.dot(layer_in, query_weight, preferred_element_type=jnp.float32).astype(
        jnp.bfloat16
    )
    keys_own = jnp.dot(layer_in, key_weight, preferred_element_type=jnp.float32).astype(
        jnp.bfloat16
    )
    values_own = jnp.dot(layer_in, value_weight, preferred_element_type=jnp.float32).astype(
        jnp.bfloat16
    )
    query_heads = queries.reshape(span_rows, head_count, HEAD_DIM)
    initial = (
        jnp.full((head_count, span_rows), MASKED, jnp.float32),
        jnp.zeros((head_count, span_rows), jnp.float32),
        jnp.zeros((head_count, span_rows, HEAD_DIM), jnp.float32),
    )
    fold_state = initial
    key_piece = lax.all_gather(keys_own, "ctx", axis=0, tiled=True)
    value_piece = lax.all_gather(values_own, "ctx", axis=0, tiled=True)
    piece_rows = key_piece.shape[0]
    block_rows = math.gcd(piece_rows, span_rows)
    key_blocks = key_piece.reshape(piece_rows // block_rows, block_rows, head_count, HEAD_DIM)
    value_blocks = value_piece.reshape(piece_rows // block_rows, block_rows, head_count, HEAD_DIM)

    def step_block(block_state, block_item):
        running_max, running_sum, accumulated = block_state
        key_block, value_block, block_index = block_item
        key_keep = lax.dynamic_slice_in_dim(keep_all, block_index * block_rows, block_rows)
        scores = (
            jnp.einsum("qhe,khe->hqk", query_heads, key_block, preferred_element_type=jnp.float32)
            * SCORE_SCALE
        )
        scores = jnp.where(key_keep[None, None, :], scores, MASKED)
        new_max = jnp.maximum(running_max, jnp.max(scores, axis=-1))
        factor = jnp.exp(running_max - new_max)
        soft_weights = jnp.where(key_keep[None, None, :], jnp.exp(scores - new_max[..., None]), 0.0)
        running_sum = running_sum * factor + jnp.sum(soft_weights, axis=-1)
        accumulated = accumulated * factor[..., None] + jnp.einsum(
            "hqk,khe->hqe",
            soft_weights.astype(jnp.bfloat16),
            value_block,
            preferred_element_type=jnp.float32,
        )
        return ((new_max, running_sum, accumulated), None)

    block_indices = jnp.arange(piece_rows // block_rows, dtype=jnp.int32)
    fold_state, unused = lax.scan(step_block, fold_state, (key_blocks, value_blocks, block_indices))
    run_max, run_sum, accumulated = fold_state
    log_total = run_max + jnp.log(run_sum)
    attn_full = jnp.transpose(accumulated / run_sum[..., None], (1, 0, 2)).reshape(
        span_rows, model_width
    )
    attn_low = attn_full.astype(jnp.bfloat16)
    gain_first32 = gain_first.astype(jnp.float32)
    gain_second32 = gain_second.astype(jnp.float32)
    branch = jnp.dot(attn_low, out_weight, preferred_element_type=jnp.float32)
    normed, normal_first, inverse_first = norm_forward(
        layer_in.astype(jnp.float32) + branch, gain_first32
    )
    normed_low = normed.astype(jnp.bfloat16)
    upward = jnp.dot(normed_low, up_weight, preferred_element_type=jnp.float32)
    active, gelu_pull = jax.vjp(gelu_exact, upward)
    active_low = active.astype(jnp.bfloat16)
    down_out = jnp.dot(active_low, down_weight, preferred_element_type=jnp.float32)
    result, normal_second, inverse_second = norm_forward(normed + down_out, gain_second32)
    result_low = result.astype(jnp.bfloat16)
    arrived = lax.all_to_all(result_low, "ctx", split_axis=0, concat_axis=0, tiled=True)
    sources = (
        jnp.arange(ctx_count, dtype=jnp.int32)[:, None] * span_rows
        + ctx_rank * per_peer
        + jnp.arange(per_peer, dtype=jnp.int32)[None, :]
    ).reshape(span_rows)
    local_pos = jnp.take(dealt_order, sources) - ctx_rank * span_rows
    in_order = jnp.zeros_like(arrived).at[local_pos].set(arrived)
    target = teacher[0].astype(jnp.float32)
    live_rows = (ctx_rank * span_rows + jnp.arange(span_rows, dtype=jnp.int32) < length)[:, None]
    residual_err = jnp.where(live_rows, in_order.astype(jnp.float32) - target, 0.0)
    total_sq = lax.psum(jnp.sum(residual_err * residual_err), ("dp", "ctx"))
    valid_total = valid_count[0].astype(jnp.float32)
    loss_value = (total_sq / (2.0 * model_width * valid_total)).reshape(1)
    grad_scale = seq_len * dp_count / valid_total
    grad_order = (residual_err * grad_scale).astype(jnp.bfloat16)
    outgoing = jnp.take(grad_order, local_pos, axis=0)
    grad_result = lax.all_to_all(outgoing, "ctx", split_axis=0, concat_axis=0, tiled=True).astype(
        jnp.float32
    )
    grad_sum_second, grad_gain_second = norm_backward(
        grad_result, gain_second32, normal_second, inverse_second
    )
    down_grad_low = grad_sum_second.astype(jnp.bfloat16)
    grad_down_w = row_product(active_low, down_grad_low)
    grad_active = by_transpose(down_grad_low, down_weight)
    grad_upward = gelu_pull(grad_active)[0].astype(jnp.bfloat16)
    grad_up_w = row_product(normed_low, grad_upward)
    grad_normed = grad_sum_second + by_transpose(grad_upward, up_weight)
    grad_hidden, grad_gain_first = norm_backward(
        grad_normed, gain_first32, normal_first, inverse_first
    )
    branch_grad = grad_hidden.astype(jnp.bfloat16)
    grad_out_w = row_product(attn_low, branch_grad)
    attn_grad_low = by_transpose(branch_grad, out_weight).astype(jnp.bfloat16)
    grad_heads = attn_grad_low.reshape(span_rows, head_count, HEAD_DIM)
    row_delta = jnp.sum(
        (attn_grad_low.astype(jnp.float32) * attn_full).reshape(span_rows, head_count, HEAD_DIM),
        axis=-1,
    ).T
    keys_all, values_all = (
        lax.all_gather(keys_own, "ctx", axis=0, tiled=True),
        lax.all_gather(values_own, "ctx", axis=0, tiled=True),
    )
    blocks_count = seq_len // span_rows
    key_stack = keys_all.reshape(blocks_count, span_rows, head_count, HEAD_DIM)
    value_stack = values_all.reshape(blocks_count, span_rows, head_count, HEAD_DIM)

    def score_terms(
        query_block, grad_block, total_block, delta_block, key_block, value_block, key_keep
    ):
        scores = (
            jnp.einsum("qhe,khe->hqk", query_block, key_block, preferred_element_type=jnp.float32)
            * SCORE_SCALE
        )
        soft_weights = jnp.where(
            key_keep[None, None, :], jnp.exp(scores - total_block[..., None]), 0.0
        )
        prob_grad = jnp.einsum(
            "qhe,khe->hqk", grad_block, value_block, preferred_element_type=jnp.float32
        )
        score_grad = (soft_weights * (prob_grad - delta_block[..., None])).astype(jnp.bfloat16)
        return (soft_weights, score_grad)

    def back_block(query_grad, block_item):
        key_block, value_block, block_index = block_item
        key_keep = lax.dynamic_slice_in_dim(keep_all, block_index * span_rows, span_rows)
        soft_weights, score_grad = score_terms(
            query_heads, grad_heads, log_total, row_delta, key_block, value_block, key_keep
        )
        value_grad = jnp.einsum(
            "hqk,qhe->khe",
            soft_weights.astype(jnp.bfloat16),
            grad_heads,
            preferred_element_type=jnp.float32,
        )
        query_grad = query_grad + SCORE_SCALE * jnp.einsum(
            "hqk,khe->qhe", score_grad, key_block, preferred_element_type=jnp.float32
        )
        key_grad = SCORE_SCALE * jnp.einsum(
            "hqk,qhe->khe", score_grad, query_heads, preferred_element_type=jnp.float32
        )
        return (query_grad, (key_grad, value_grad))

    query_grad, (key_grads, value_grads) = lax.scan(
        back_block,
        jnp.zeros((span_rows, head_count, HEAD_DIM), jnp.float32),
        (key_stack, value_stack, jnp.arange(blocks_count, dtype=jnp.int32)),
    )
    key_grad_sum, value_grad_sum = (
        lax.psum_scatter(
            key_grads.reshape(seq_len, model_width).astype(jnp.bfloat16),
            "ctx",
            scatter_dimension=0,
            tiled=True,
        ).astype(jnp.float32),
        lax.psum_scatter(
            value_grads.reshape(seq_len, model_width).astype(jnp.bfloat16),
            "ctx",
            scatter_dimension=0,
            tiled=True,
        ).astype(jnp.float32),
    )
    query_grad_low = query_grad.reshape(span_rows, model_width).astype(jnp.bfloat16)
    key_grad_low = key_grad_sum.astype(jnp.bfloat16)
    value_grad_low = value_grad_sum.astype(jnp.bfloat16)
    grad_query_w = row_product(layer_in, query_grad_low)
    grad_key_w = row_product(layer_in, key_grad_low)
    grad_value_w = row_product(layer_in, value_grad_low)
    token_grad = (
        grad_hidden
        + by_transpose(query_grad_low, query_weight)
        + by_transpose(key_grad_low, key_weight)
        + by_transpose(value_grad_low, value_weight)
    )
    up_part, down_part, second_part = (
        lax.psum_scatter(
            grad_up_w.astype(jnp.bfloat16), "dp", scatter_dimension=0, tiled=True
        ).astype(jnp.float32),
        lax.psum_scatter(
            grad_down_w.astype(jnp.bfloat16), "dp", scatter_dimension=0, tiled=True
        ).astype(jnp.float32),
        lax.psum_scatter(
            grad_gain_second.astype(jnp.bfloat16), "dp", scatter_dimension=0, tiled=True
        ).astype(jnp.float32),
    )
    query_part, key_part, value_part, out_part, first_part = (
        lax.psum_scatter(
            grad_query_w.astype(jnp.bfloat16), "dp", scatter_dimension=0, tiled=True
        ).astype(jnp.float32),
        lax.psum_scatter(
            grad_key_w.astype(jnp.bfloat16), "dp", scatter_dimension=0, tiled=True
        ).astype(jnp.float32),
        lax.psum_scatter(
            grad_value_w.astype(jnp.bfloat16), "dp", scatter_dimension=0, tiled=True
        ).astype(jnp.float32),
        lax.psum_scatter(
            grad_out_w.astype(jnp.bfloat16), "dp", scatter_dimension=0, tiled=True
        ).astype(jnp.float32),
        lax.psum_scatter(
            grad_gain_first.astype(jnp.bfloat16), "dp", scatter_dimension=0, tiled=True
        ).astype(jnp.float32),
    )
    summed = (
        lax.psum(query_part.astype(jnp.bfloat16), "ctx").astype(jnp.float32),
        lax.psum(key_part.astype(jnp.bfloat16), "ctx").astype(jnp.float32),
        lax.psum(value_part.astype(jnp.bfloat16), "ctx").astype(jnp.float32),
        lax.psum(out_part.astype(jnp.bfloat16), "ctx").astype(jnp.float32),
        lax.psum(up_part.astype(jnp.bfloat16), "ctx").astype(jnp.float32),
        lax.psum(down_part.astype(jnp.bfloat16), "ctx").astype(jnp.float32),
        lax.psum(first_part.astype(jnp.bfloat16), "ctx").astype(jnp.float32),
        lax.psum(second_part.astype(jnp.bfloat16), "ctx").astype(jnp.float32),
    )
    query_sum, key_sum, value_sum, out_sum, up_sum, down_sum, first_sum, second_sum = summed
    return (
        in_order[None],
        loss_value,
        token_grad[None],
        query_sum,
        key_sum,
        value_sum,
        out_sum,
        up_sum,
        down_sum,
        first_sum,
        second_sum,
    )


class Place:
    def __init__(self):
        dp = lax.axis_index("dp")
        self.x = lax.axis_index("ctx")
        self.z, self.y, self.c = dp // 4, (dp // 2) % 2, dp % 2
        self.xo, self.yo, self.co = 1 - self.x, 1 - self.y, 1 - self.c
        self.to_x = (dp, self.xo)
        self.to_y = (self.z * 4 + self.yo * 2 + self.c, self.x)
        self.to_c = (self.z * 4 + self.y * 2 + self.co, self.x)
        self.z_up = [(self.z + k) % 4 for k in range(4)]
        self.z_down = [(self.z + 4 - k) % 4 for k in range(4)]
        self.to_z = [(self.z_up[k] * 4 + self.y * 2 + self.c, self.x) for k in range(4)]

    def barrier(self):
        semaphore = pltpu.get_barrier_semaphore()
        for partner in [self.to_x, self.to_y, self.to_c] + self.to_z[1:]:
            pl.semaphore_signal(semaphore, inc=1, device_id=partner, device_id_type=MESH)
        pl.semaphore_wait(semaphore, 6)


class Copy:
    def __init__(self, refs, send, at, recv, to, partner):
        self.refs, self.send, self.at, self.recv, self.to = refs, send, at, recv, to
        self.partner = partner

    def make(self):
        src, dst = self.refs()
        return pltpu.make_async_remote_copy(
            src_ref=src,
            dst_ref=dst,
            send_sem=self.send.at[self.at],
            recv_sem=self.recv.at[self.to],
            device_id=self.partner,
            device_id_type=MESH,
        )

    def wait_send(self):
        self.make().wait_send()

    def wait_recv(self):
        self.make().wait_recv()


class Links:
    def __init__(self, send, recv):
        self.send, self.recv, self.used, self.flying = send, recv, 0, []
        self.free = list(range(send.shape[0]))

    def start(self, refs, partner):
        if not self.free:
            self.sent(self.flying[0][0])
        at = self.free.pop(0)
        copy = Copy(refs, self.send, at, self.recv, self.used, partner)
        self.used += 1
        copy.make().start()
        self.flying.append((copy, at))
        return copy

    def sent(self, copy):
        for entry in list(self.flying):
            if entry[0] is copy:
                copy.wait_send()
                self.free.append(entry[1])
        self.flying = [entry for entry in self.flying if entry[0] is not copy]

    def drain(self):
        for copy, at in list(self.flying):
            self.sent(copy)


class Gather:
    def __init__(self, block, early, shard, shift, whole, place, links, own_sem):
        first, last, self.split, self.col0, self.width = block
        self.early = early
        self.rows = pl.ds(first, last - first)
        self.shard, self.shift, self.whole = shard, shift, whole
        self.p, self.links = place, links
        self.own_sem = own_sem
        self.mine, self.theirs = self.half(place.x), self.half(place.xo)
        self.source = self.half(place.x, shift)
        self.last = 4 if self.split else 3

    def cols(self, shift=0):
        return pl.ds(self.col0 + shift, self.width)

    def half(self, x, shift=0):
        if not self.split:
            return self.cols(shift)
        size = self.width // 2
        return pl.ds(pl.multiple_of(self.col0 + shift + x * size, 128), size)

    def piece(self, z, y, cols):
        return self.whole.at[z, y, self.p.c, self.rows, cols]

    def own(self):
        p = self.p
        return pltpu.make_async_copy(
            self.shard.at[:, self.cols(self.shift)], self.piece(p.z, p.y, self.cols()), self.own_sem()
        )

    def push(self, z, y, cols, partner):
        return self.links.start(lambda: (self.piece(z, y, cols),) * 2, partner)

    def send_own(self, partner):
        p = self.p
        return self.links.start(
            lambda: (self.shard.at[:, self.source], self.piece(p.z, p.y, self.mine)), partner
        )

    def step0(self):
        p = self.p
        self.from_z = [self.send_own(p.to_z[k]) for k in range(1, 4)]
        self.own().start()
        if self.early:
            self.own_y()

    def own_y(self):
        self.from_y = [self.send_own(self.p.to_y)]

    def step1(self):
        p = self.p
        if not self.early:
            self.own_y()
        self.from_x = []
        for k in range(1, 4):
            self.from_z[k - 1].wait_recv()
            piece = (p.z_down[k], p.y, self.mine)
            self.from_y.append(self.push(*piece, p.to_y))
            if self.split:
                self.from_x.append(self.push(*piece, p.to_x))
        self.own().wait()
        self.from_c = [self.push(slice(None), p.y, self.mine, p.to_c)]

    def step2(self):
        p, every = self.p, slice(None)
        for copy in self.from_y:
            copy.wait_recv()
        if self.split:
            self.across = self.push(every, p.yo, self.mine, p.to_x)
        self.from_c.append(self.push(every, p.yo, self.mine, p.to_c))
        if self.split:
            for copy in self.from_x:
                copy.wait_recv()
            self.from_c.append(self.push(every, p.y, self.theirs, p.to_c))

    def step3(self):
        if self.split:
            self.across.wait_recv()
            self.from_c.append(self.push(slice(None), self.p.yo, self.theirs, self.p.to_c))
        else:
            self.step4()

    def step4(self):
        for copy in self.from_c:
            copy.wait_recv()


class Reduce:
    def __init__(self, block, at, grads, out, out0, shift, place, links, here, core_in, bufs):
        first, last, self.split, self.col0, self.width = block
        self.rows = last - first
        self.at0, self.here0, self.out0, self.shift = at, here, out0, shift
        self.at, self.here = pl.ds(at, self.rows), pl.ds(here, self.rows)
        self.grads, self.out = grads, out
        self.p, self.links = place, links
        self.core_in, self.bufs = core_in, bufs
        limit = 32 * 768 // self.width
        self.block = max(b for b in range(16, min(self.rows, limit) + 1, 16) if self.rows % b == 0)
        self.stage = 0
        self.mine, self.theirs = self.half(place.x), self.half(place.xo)
        self.out_mine = self.half(place.x, shift)
        self.last = 5 if self.split else 4

    def cols(self, shift=0):
        return pl.ds(self.col0 + shift, self.width)

    def half(self, x, shift=0):
        if not self.split:
            return self.cols(shift)
        size = self.width // 2
        return pl.ds(pl.multiple_of(self.col0 + shift + x * size, 128), size)

    def low(self):
        return pl.ds(self.col0, self.width // 2)

    def high(self):
        return pl.ds(self.col0 + self.width // 2, self.width // 2) if self.split else self.cols()

    def add(self, outer, target, source):
        steps = self.rows // self.block

        def body(i, carry):
            first = pl.multiple_of((i % steps) * self.block, 16)
            put = target(i // steps, pl.ds(self.at0 + first, self.block))
            given = source(i // steps, pl.ds(self.here0 + first, self.block))
            self.grads[put] = (
                self.grads[put].astype(jnp.float32) + given.astype(jnp.float32)
            ).astype(jnp.bfloat16)
            return carry

        lax.fori_loop(0, outer * steps, body, 0)

    def step0(self):
        p = self.p
        self.by_core = self.links.start(
            lambda: (
                self.grads.at[:, :, p.co, self.at, self.cols()],
                self.core_in().at[:, :, self.here, self.cols()],
            ),
            p.to_c,
        )

    def add_core(self, y):
        p = self.p
        self.add(
            4,
            lambda i, rows: (i, y, p.c, rows, self.cols()),
            lambda i, rows: self.core_in()[i, y, rows, self.cols()],
        )

    def send_y(self):
        p = self.p
        self.by_y = self.links.start(
            lambda: (
                self.grads.at[:, p.yo, p.c, self.at, self.mine],
                self.bufs(0, slice(None)).at[:, self.here, self.high()],
            ),
            p.to_y,
        )

    def step1(self):
        p = self.p
        self.by_core.wait_recv()
        self.add_core(p.yo)
        if not self.split:
            self.send_y()
        self.add_core(p.y)
        if self.split:
            self.by_x = [self.send_x(0, p.yo), self.send_x(1, p.y)]

    def send_x(self, i, y):
        p = self.p
        return self.links.start(
            lambda: (
                self.grads.at[:, y, p.c, self.at, self.theirs],
                self.bufs(i, slice(None)).at[:, self.here, self.low()],
            ),
            p.to_x,
        )

    def add_x(self, i, y):
        p = self.p
        self.by_x[i].wait_recv()
        self.add(
            4,
            lambda j, rows: (j, y, p.c, rows, self.mine),
            lambda j, rows: self.bufs(i, j)[rows, self.low()],
        )

    def step2(self):
        if self.split:
            self.add_x(0, self.p.yo)
            self.send_y()
            self.add_x(1, self.p.y)
        else:
            self.reduce_y()

    def reduce_y(self):
        p = self.p
        self.by_y.wait_recv()
        self.add(
            4,
            lambda i, rows: (i, p.y, p.c, rows, self.mine),
            lambda i, rows: self.bufs(0, i)[rows, self.high()],
        )
        self.by_z = [self.send_z(k) for k in range(1, 4)]

    def send_z(self, k):
        p = self.p
        return self.links.start(
            lambda: (
                self.grads.at[p.z_up[k], p.y, p.c, self.at, self.mine],
                self.bufs(1, k - 1).at[self.here, self.high()],
            ),
            p.to_z[k],
        )

    def reduce_z(self, put):
        p = self.p
        for copy in self.by_z:
            copy.wait_recv()

        def body(i, carry):
            first = pl.multiple_of(i * self.block, 16)
            rows = pl.ds(self.here0 + first, self.block)
            place = (p.z, p.y, p.c, pl.ds(self.at0 + first, self.block), self.mine)
            total = self.grads[place].astype(jnp.float32)
            for k in range(3):
                total = total + self.bufs(1, k)[rows, self.high()].astype(jnp.float32)
            put(pl.ds(self.out0 + first, self.block), place, total.astype(jnp.bfloat16))
            return carry

        lax.fori_loop(0, self.rows // self.block, body, 0)

    def step3(self):
        p = self.p
        if self.split:
            self.reduce_y()
            return

        def put(rows, place, value):
            self.grads[place] = value

        self.reduce_z(put)
        self.by_x = self.links.start(
            lambda: (
                self.grads.at[p.z, p.y, p.c, self.at, self.cols()],
                self.bufs(1, 3).at[self.here, self.cols()],
            ),
            p.to_x,
        )

    def step4(self):
        p = self.p
        if self.split:

            def put(rows, place, value):
                self.out[rows, self.out_mine] = value

            self.reduce_z(put)
            self.by_x = self.links.start(
                lambda: (self.out.at[pl.ds(self.out0, self.rows), self.out_mine],) * 2, p.to_x
            )
            return
        self.by_x.wait_recv()

        def body(i, carry):
            first = pl.multiple_of(i * self.block, 16)
            rows = pl.ds(self.here0 + first, self.block)
            own = self.grads[p.z, p.y, p.c, pl.ds(self.at0 + first, self.block), self.cols()]
            self.out[pl.ds(self.out0 + first, self.block), self.cols(self.shift)] = (
                own.astype(jnp.float32) + self.bufs(1, 3)[rows, self.cols()].astype(jnp.float32)
            ).astype(jnp.bfloat16)
            return carry

        lax.fori_loop(0, self.rows // self.block, body, 0)

    def step5(self):
        self.by_x.wait_recv()

    def beat(self):
        getattr(self, "step" + str(self.stage))()
        self.stage += 1


class Total:
    last = 4

    def __init__(self, value, core_in, x_in, y_in, by_z, place, links):
        self.value, self.core_in, self.x_in, self.y_in, self.by_z = value, core_in, x_in, y_in, by_z
        self.p, self.links = place, links
        self.stage = 0

    def step0(self):
        self.copy = self.links.start(lambda: (self.value.at[0], self.core_in), self.p.to_c)

    def step1(self):
        self.copy.wait_recv()
        self.value[1] = self.value[0] + self.core_in[...]
        self.copy = self.links.start(lambda: (self.value.at[1], self.x_in), self.p.to_x)

    def step2(self):
        self.copy.wait_recv()
        self.value[2] = self.value[1] + self.x_in[...]
        self.copy = self.links.start(lambda: (self.value.at[2], self.y_in), self.p.to_y)

    def step3(self):
        self.copy.wait_recv()
        z = self.p.z
        self.by_z[z] = self.value[2] + self.y_in[...]
        self.spread = [
            self.links.start(lambda: (self.by_z.at[z],) * 2, self.p.to_z[k]) for k in range(1, 4)
        ]

    def step4(self):
        for copy in self.spread:
            copy.wait_recv()

    def sum(self):
        return ((self.by_z[0] + self.by_z[1]) + self.by_z[2]) + self.by_z[3]

    def beat(self):
        getattr(self, "step" + str(self.stage))()
        self.stage += 1


ROOT_HALF = 0.7071067811865476
DENSITY = 0.3989422804014327


def dot(left, right):
    return jnp.dot(left, right, preferred_element_type=jnp.float32)


def turned(left, right):
    return lax.dot_general(
        left, right, (((0,), (0,)), ((), ())), preferred_element_type=jnp.float32
    )


def by_turned(left, right):
    return lax.dot_general(
        left, right, (((1,), (1,)), ((), ())), preferred_element_type=jnp.float32
    )


def layer_kernel(s, *refs):
    tokens, teacher, order_row, length, valid = refs[:5]
    weights, (ordered_out, total_out, token_out), outs = refs[5:11], refs[11:14], refs[14:18]
    refs = refs[8:]
    (W, G, tok, QKV, dO, stat, attn, n1, r1, low1, act, gp, acc, teach, res_in, low2, gains, sums) = refs[10:28]
    total_refs, (send, recv, local), (order_col, core_in, bufs) = refs[28:33], refs[33:36], refs[36:]
    qs, ks, vs = QKV.at[0], QKV.at[1], QKV.at[2]
    f32, bf16 = jnp.float32, jnp.bfloat16
    span, width, shard, downs = s.span, s.width, s.shard, s.downs
    pairs = width // 128
    third = width // 3
    place = Place()
    x, xo = place.x, place.xo
    links = Links(send, recv)

    def own(first, size):
        return pl.ds(pl.multiple_of(x * span + first, 16), size)

    def other(first, size):
        return pl.ds(pl.multiple_of(xo * span + first, 16), size)

    def loop(count, body):
        def step(i, carry):
            body(i)
            return carry

        lax.fori_loop(0, count, step, 0)

    def each(i, count, action):
        for k in range(count):
            pl.when(i == k)(lambda: action())

    def matrix(first):
        return W[:, :, :, pl.ds(pl.multiple_of(first, 16), shard), :].reshape(width, width)

    def semaphore(i):
        return local.at[i]

    gathers = [
        Gather(block, i < s.early, weights[j], shift, W, place, links, functools.partial(semaphore, i))
        for i, (block, (j, shift)) in enumerate(zip(s.gather_blocks, s.sources))
    ]
    n_gather = len(gathers)
    stages = [0] * n_gather
    forward = iter(s.forward)

    def advance():
        for i in next(forward):
            getattr(gathers[i], "step" + str(stages[i]))()
            stages[i] += 1

    def arrived(*blocks):
        advance()
        assert all(stages[i] > gathers[i].last for i in blocks)

    place.barrier()
    own_tokens = pltpu.make_async_copy(tokens, tok.at[own(0, span)], local.at[n_gather])
    own_tokens.start()
    own_teacher = pltpu.make_async_copy(teacher, gp.at[0], local.at[n_gather + 1])
    own_teacher.start()
    send_tokens = links.start(lambda: (tokens, tok.at[own(0, span)]), place.to_x)
    advance()
    order_col[...] = jnp.broadcast_to(order_row[...].astype(f32), (128, 2 * span)).T
    length_now = length[0]
    length_float = length_now.astype(f32)
    iota_rows = lax.broadcasted_iota(jnp.int32, (s.block, span), 1)

    def pick(c):
        rows = pl.ds(pl.multiple_of(c * span + x * s.block, 16), s.block)
        position = order_col[rows, :].astype(jnp.int32) - x * span
        chosen = iota_rows == jnp.concatenate([position] * (span // 128), axis=1)
        return jnp.where(chosen, 1.0, 0.0).astype(bf16)

    own_teacher.wait()
    for n in range(3):
        cols = slice(n * third, (n + 1) * third)
        gp[1, : s.block, cols] = dot(pick(xo), gp[0, :, cols]).astype(bf16)
        teach[x, :, cols] = dot(pick(x), gp[0, :, cols]).astype(bf16)
    teach_copy = links.start(lambda: (gp.at[1, pl.ds(0, s.block)], teach.at[x]), place.to_x)
    advance()
    arrived(0, 1, 2)

    own_tokens.wait()

    def side(i):
        @pl.when(i == 1)
        def _():
            send_tokens.wait_recv()

        rows = pl.ds(pl.multiple_of(jnp.where(i == 0, x, xo) * span, 16), span)

        def project(j):
            scale = jnp.where(j == 0, SCORE_SCALE, 1.0)
            QKV[j, rows, :] = (dot(tok[rows, :], matrix(j * shard)) * scale).astype(bf16)

        loop(3, project)
        each(i, 2, advance)

    loop(2, side)

    lane = lax.broadcasted_iota(jnp.int32, (1, 128), 1)
    even32 = lane < HEAD_DIM
    even = jnp.where(even32, 1.0, 0.0).astype(bf16)
    odd = jnp.where(even32, 0.0, 1.0).astype(bf16)
    bias_row = jnp.where(order_row[0:1, :] < length_now, 0.0, MASKED)

    def attend(pair):
        lanes = pl.ds(pl.multiple_of(pair * 128, 128), 128)
        query, key, value = qs[own(0, span), lanes], ks[:, lanes], vs[:, lanes]
        tops, mixed = [], []
        for keep, rest in ((even, odd), (odd, even)):
            scores = by_turned(query * keep, key) + bias_row
            top = jnp.max(scores, axis=1, keepdims=True)
            weight = jnp.exp(scores - top).astype(bf16)
            tops.append(top)
            mixed.append(dot(weight, value * keep + rest))
        part = jnp.where(even32, mixed[0], mixed[1])
        total = pltpu.roll(jnp.where(even32, mixed[1], mixed[0]), HEAD_DIM, 1)
        attn[:, lanes] = (part / total).astype(bf16)
        log_rows = (jnp.where(even32, tops[0], tops[1]) + jnp.log(total)).T
        for h in range(2):
            stat[x, 0, pl.ds(2 * pair + h, 1), :] = log_rows[
                h * HEAD_DIM : h * HEAD_DIM + 1, :
            ]
        each(pair, pairs, advance)

    loop(pairs, attend)

    arrived(3)
    device = lax.broadcasted_iota(jnp.int32, (16, width), 0)
    feature = lax.broadcasted_iota(jnp.int32, (16, width), 1)
    mine = (feature // shard) == device
    spread = jnp.where(
        lax.broadcasted_iota(jnp.int32, (128, width), 1) % shard
        == lax.broadcasted_iota(jnp.int32, (128, width), 0),
        1.0,
        0.0,
    ).astype(bf16)
    gain_rows = W[:, :, :, s.gain0 : s.gain0 + 16, :128].reshape(16, 16, 128).astype(f32)
    for g in range(2):
        wide = dot(gain_rows[:, g, :].astype(bf16), spread)
        gains[g : g + 1, :] = jnp.sum(jnp.where(mine, wide, 0.0), axis=0, keepdims=True)

    acc[...] = dot(attn[...], matrix(s.out0))
    advance()
    rows_n = s.rows_n

    def wide_column(column):
        return jnp.broadcast_to(column, (rows_n, 128))

    def first_norm(b):
        first = pl.multiple_of(b * rows_n, 16)
        rows = pl.ds(first, rows_n)
        hidden = tok[own(first, rows_n), :].astype(f32) + acc[rows, :]
        center = hidden - jnp.mean(hidden, axis=1, keepdims=True)
        inverse = lax.rsqrt(jnp.mean(center * center, axis=1, keepdims=True) + EPSILON)
        normal = center * inverse
        n1[rows, :] = normal
        r1[rows, :] = wide_column(inverse)
        low1[rows, :] = (normal * gains[0:1, :]).astype(bf16)

    loop(span // rows_n, first_norm)
    advance()

    teach_copy.wait_recv()
    links.sent(teach_copy)

    def ahead(i, count):
        steps = iter(range(count))

        def action():
            if next(steps) > 0:
                advance()
            advance()

        each(i, count, action)

    def upward(p):
        ahead(p, s.panels)
        rows = pl.ds(pl.multiple_of(s.up0 + p * shard, 16), shard)
        for n in range(3):
            cols = slice(n * third, (n + 1) * third)
            value = dot(low1[...], W[:, :, :, rows, cols].reshape(width, third))
            cdf = 0.5 * (1.0 + lax.erf(value * ROOT_HALF))
            act[p, :, cols] = (value * cdf).astype(bf16)
            gp[p, :, cols] = (cdf + value * (jnp.exp(-0.5 * value * value) * DENSITY)).astype(bf16)

    def downward(n):
        ahead(n, 3)
        cols = pl.ds(pl.multiple_of(n * third, 128), third)
        value = None
        for p in range(s.panels):
            part = dot(act[p], W[p, :, :, s.down0 :, cols].reshape(width, third))
            value = part if value is None else value + part
        acc[:, cols] = value

    loop(s.panels, upward)
    advance()
    loop(3, downward)
    advance()
    assert all(stage > item.last for stage, item in zip(stages, gathers))

    sums[...] = jnp.zeros_like(sums)
    valid_total = jnp.full((1, 1), valid[0], jnp.int32).astype(f32)
    grad_scale = s.tokens / valid_total

    def fold(values):
        return jnp.sum(values.reshape(rows_n // 8, 8, width), axis=0)

    def second_norm(b):
        first = pl.multiple_of(b * rows_n, 16)
        rows = pl.ds(first, rows_n)
        hidden = n1[rows, :] * gains[0:1, :] + acc[rows, :]
        center = hidden - jnp.mean(hidden, axis=1, keepdims=True)
        inverse = lax.rsqrt(jnp.mean(center * center, axis=1, keepdims=True) + EPSILON)
        normal = center * inverse
        gain = gains[1:2, :]
        result = (normal * gain).astype(bf16)
        per = s.block // rows_n
        at = pl.ds(pl.multiple_of((b % per) * rows_n, 16), rows_n)
        target = teach[b // per, at, :].astype(f32)
        teach[b // per, at, :] = result
        live = order_col[own(first, rows_n), 0:1] < length_float
        error = jnp.where(live, result.astype(f32) - target, 0.0)
        sums[2] += fold(error * error)
        grad = (error * grad_scale).astype(bf16).astype(f32)
        sums[1] += fold(grad * normal)
        scaled = grad * gain
        grad_sum = inverse * (
            scaled
            - jnp.mean(scaled, axis=1, keepdims=True)
            - normal * jnp.mean(scaled * normal, axis=1, keepdims=True)
        )
        acc[rows, :] = grad_sum
        low2[rows, :] = grad_sum.astype(bf16)

    loop(span // rows_n, second_norm)
    links.drain()
    send_result = links.start(lambda: (teach.at[xo], res_in), place.to_x)
    total_refs[0][0] = jnp.broadcast_to(
        jnp.sum(jnp.sum(sums[2], axis=0, keepdims=True), axis=1, keepdims=True), (8, 128)
    )
    total = Total(*total_refs, place, links)

    reduces = [total]
    backward = iter(s.backward)

    def beat():
        for i in next(backward):
            reduces[i].beat()

    def prepare(block, out, shift=0, in_weights=False):
        first = block[0]
        return Reduce(
            block,
            first + s.down0 if in_weights else first - s.out0,
            W if in_weights else G,
            outs[out],
            first if in_weights else 0,
            shift,
            place,
            links,
            first + s.up0 if in_weights else first - s.out0,
            (lambda: W.at[:, :, 0]) if in_weights else (lambda: core_in),
            (lambda h, j: W.at[j, h, 1]) if in_weights else (lambda h, j: bufs.at[h, j]),
        )

    coming = [prepare(block, 3) for block in s.down_blocks]
    coming += [prepare(block, 2, p * width) for p, block in enumerate(s.up_blocks)]
    coming += [prepare(s.out_block, 1)]
    coming += [prepare(block, 0, in_weights=True) for block in s.last_blocks]

    def enter():
        reduces.append(coming.pop(0))
        beat()

    def panel_grad(first, left, right):
        value = turned(left[...], right[...]).astype(bf16)
        at = pl.ds(pl.multiple_of(first - s.out0, 16), shard)
        G[:, :, :, at, :] = value.reshape(4, 2, 2, shard, width)

    def down_grad(n):
        cols = pl.ds(pl.multiple_of(n * third, 128), third)

        def panel(p):
            value = turned(act[p], low2[:, cols]).astype(bf16)
            G[p, :, :, s.down0 - s.out0 :, cols] = value.reshape(2, 2, downs, third)

        loop(s.panels, panel)
        each(n, 3, enter)

    def up_grad(p):
        value = by_turned(low2[...], W[p, :, :, s.down0 :, :].reshape(width, width))
        gp[p] = (value * gp[p].astype(f32)).astype(bf16)
        panel_grad(s.up0 + p * shard, low1, gp.at[p])
        each(p, s.panels, enter)

    def normed_grad(p):
        acc[...] += by_turned(gp[p], matrix(s.up0 + p * shard))

    loop(3, down_grad)
    loop(s.panels, up_grad)
    loop(s.panels, normed_grad)
    beat()

    def first_back(b):
        rows = pl.ds(pl.multiple_of(b * rows_n, 16), rows_n)
        grad, normal = acc[rows, :], n1[rows, :]
        sums[0] += fold(grad * normal)
        scaled = grad * gains[0:1, :]
        hidden_grad = r1[rows, 0:1] * (
            scaled
            - jnp.mean(scaled, axis=1, keepdims=True)
            - normal * jnp.mean(scaled * normal, axis=1, keepdims=True)
        )
        acc[rows, :] = hidden_grad
        low2[rows, :] = hidden_grad.astype(bf16)

    loop(span // rows_n, first_back)
    beat()

    dO[...] = by_turned(low2[...], matrix(s.out0)).astype(bf16)
    head = lax.broadcasted_iota(jnp.int32, (16, width), 0)
    in_head = jnp.where((feature // HEAD_DIM) == head, 1.0, 0.0)

    def head_delta(b):
        first = pl.multiple_of(b * 128, 128)
        rows = pl.ds(first, 128)
        product = dO[rows, :].astype(f32) * attn[rows, :].astype(f32)
        stat[x, 1, :, rows] = lax.dot_general(
            in_head,
            product,
            (((1,), (1,)), ((), ())),
            precision=lax.Precision.HIGHEST,
            preferred_element_type=f32,
        )

    loop(span // 128, head_delta)
    send_grad = links.start(lambda: (dO, tok.at[own(0, span)]), place.to_x)
    send_stat = links.start(lambda: (stat.at[x],) * 2, place.to_x)

    panel_grad(s.out0, attn, low2)
    pieces = []
    for g in range(2):
        row = jnp.sum(sums[g], axis=0, keepdims=True)
        split = jnp.where(mine, jnp.broadcast_to(row, (16, width)), 0.0).astype(bf16)
        pieces.append(by_turned(split, spread))
    at_row = lax.broadcasted_iota(jnp.int32, (16, 16, 128), 1)
    gain_block = jnp.where(
        at_row == 0, pieces[0][:, None, :], jnp.where(at_row == 1, pieces[1][:, None, :], 0.0)
    ).astype(bf16)
    G[:, :, :, shard : shard + 16, :128] = gain_block.reshape(4, 2, 2, 16, 128)
    G[:, :, :, shard : shard + 16, 128:] = jnp.zeros((4, 2, 2, 16, width - 128), bf16)
    enter()

    def block_terms(key, value, bias, query, grad, log_row, delta_row):
        scores = by_turned(key, query) + bias
        p = jnp.exp(scores - log_row)
        score_grad = (p * (by_turned(value, grad) - delta_row)).astype(bf16)
        return p.astype(bf16), score_grad

    def key_side(rows, lanes):
        column = jnp.where(order_col[rows, :] < length_float, 0.0, MASKED)
        return ks[rows, lanes], vs[rows, lanes], jnp.concatenate([column] * (span // 128), axis=1)

    def pair_lanes(pair):
        return pl.ds(pl.multiple_of(pair * 128, 128), 128)

    def terms(key, value, bias, side, pair, h, keep):
        lanes = pair_lanes(pair)
        rows = pl.ds(pl.multiple_of(side * span, 16), span)
        grad = dO[:, lanes] if side is x else tok[rows, lanes]
        query, grad = qs[rows, lanes] * keep, grad * keep
        at = pl.ds(2 * pair + h, 1)
        p, score_grad = block_terms(
            key, value, bias, query, grad, stat[side, 0, at, :], stat[side, 1, at, :]
        )
        return query, grad, p, score_grad

    def back_queries(pair):
        lanes = pair_lanes(pair)
        result = to_keys = to_values = None
        for rows, mine in ((own(0, span), True), (other(0, span), False)):
            key, value, bias = key_side(rows, lanes)
            for h, keep in enumerate((even, odd)):
                query, grad, p, score_grad = terms(key, value, bias, x, pair, h, keep)
                part = turned(score_grad, key * keep)
                result = part if result is None else result + part
                if mine:
                    value_part, key_part = dot(p, grad), dot(score_grad, query)
                    to_values = value_part if to_values is None else to_values + value_part
                    to_keys = key_part if to_keys is None else to_keys + key_part
        act[0, :, lanes] = (result * SCORE_SCALE).astype(bf16)
        n1[:, lanes] = to_keys
        gp[0, :, lanes] = to_values.astype(bf16)
        each(pair, pairs, beat)

    def back_keys(pair):
        lanes = pair_lanes(pair)
        key, value, bias = key_side(own(0, span), lanes)
        to_keys, to_values = n1[:, lanes], gp[0, :, lanes].astype(f32)
        for h, keep in enumerate((even, odd)):
            query, grad, p, score_grad = terms(key, value, bias, xo, pair, h, keep)
            to_values = to_values + dot(p, grad)
            to_keys = to_keys + dot(score_grad, query)
        act[1, :, lanes] = to_keys.astype(bf16)
        act[2, :, lanes] = to_values.astype(bf16)

    def weight_grad(j, columns):
        value = turned(tok[own(0, span), :], act[j, :, columns]).astype(bf16)
        at = pl.ds(pl.multiple_of(s.down0 + j * shard, 16), shard)
        W[:, :, :, at, columns] = value.reshape(4, 2, 2, shard, value.shape[1])

    def last_pairs(i):
        loop(2, lambda k: back_keys(2 * i + k))
        columns = pl.ds(pl.multiple_of(i * 256, 128), 256)
        loop(2, lambda j: weight_grad(j + 1, columns))
        each(i, pairs // 2, enter)

    loop(pairs, back_queries)
    weight_grad(0, slice(0, width))
    enter()
    send_grad.wait_recv()
    send_stat.wait_recv()
    loop(pairs // 2, last_pairs)

    def input_grad(j):
        acc[...] += by_turned(act[j], matrix(j * shard))

    loop(3, input_grad)
    token_copy = pltpu.make_async_copy(acc, token_out, local.at[n_gather])
    token_copy.start()
    beat()
    send_result.wait_recv()

    def place_rows(n):
        cols = pl.ds(pl.multiple_of(n * third, 128), third)
        value = None
        position = lax.broadcasted_iota(jnp.int32, (span, s.block), 0) + x * span
        for c, rows in ((x, teach[x, :, cols]), (xo, res_in[:, cols])):
            at = order_row[0:1, pl.ds(pl.multiple_of(c * span + x * s.block, 128), s.block)]
            chosen = jnp.where(position == at, 1.0, 0.0).astype(bf16)
            part = dot(chosen, rows)
            value = part if value is None else value + part
        low2[:, cols] = value.astype(bf16)

    loop(3, place_rows)
    ordered_copy = pltpu.make_async_copy(low2, ordered_out, local.at[n_gather + 1])
    ordered_copy.start()
    beat()
    beat()
    assert all(item.stage > item.last for item in reduces)
    total_out[...] = total.sum()
    token_copy.wait()
    ordered_copy.wait()
    links.drain()


class Sizes:
    def __init__(self, span, width, ff, shard, downs, tokens):
        self.span, self.width, self.shard, self.downs, self.tokens = span, width, shard, downs, tokens
        self.panels = ff // width
        self.block = span // 2
        self.out0 = 3 * shard
        self.gain0 = 4 * shard
        self.up0 = self.gain0 + 16
        self.down0 = self.up0 + self.panels * shard
        self.rows = self.down0 + downs
        blocks = [(j * shard, (j + 1) * shard, 0, width) for j in range(3)]
        blocks += [(self.out0, self.up0, 0, width)]
        for p in range(self.panels):
            blocks += [(self.up0 + p * shard, self.up0 + (p + 1) * shard, 0, width)]
        third = width // 3
        blocks += [(self.down0, self.rows, n * third, third) for n in range(3)]
        self.gather_blocks = [b[:2] + (i in GATHER_SPLIT,) + b[2:] for i, b in enumerate(blocks)]
        self.sources = [(j, 0) for j in range(4)] + [(4, p * width) for p in range(self.panels)]
        self.sources += [(5, 0)] * 3
        self.early = EARLY
        back = blocks[-3:] + blocks[4:-3] + [blocks[3], blocks[0]]
        back += [(shard, self.out0, n * third, third) for n in range(3)]
        back = [b[:2] + (i in REDUCE_SPLIT,) + b[2:] for i, b in enumerate(back)]
        self.down_blocks, self.up_blocks = back[:3], back[3:-5]
        self.out_block, self.last_blocks = back[-5], back[-4:]
        self.forward, self.backward = FORWARD, BACKWARD
        self.rows_n, self.flying = 64, 64


def layer(s, *args):
    bf16, f32 = jnp.bfloat16, jnp.float32
    span, width = s.span, s.width
    both = 2 * span
    anywhere = pl.BlockSpec(memory_space=pl.ANY)
    vmem = pl.BlockSpec(memory_space=pltpu.VMEM)
    smem = pl.BlockSpec(memory_space=pltpu.SMEM)
    back = s.down_blocks + s.up_blocks + [s.out_block] + s.last_blocks
    copies = sum(15 if b[2] else 9 for b in s.gather_blocks)
    copies += sum(8 if b[2] else 6 for b in back) + 6 + 5
    small = pltpu.VMEM((8, 128), f32)
    scratch = [
        pltpu.VMEM((4, 2, 2, s.rows, width), bf16),
        pltpu.VMEM((4, 2, 2, s.rows - s.out0, width), bf16),
        pltpu.VMEM((both, width), bf16),
        pltpu.VMEM((3, both, width), bf16),
        pltpu.VMEM((span, width), bf16),
        pltpu.VMEM((2, 2, 16, span), f32),
        pltpu.VMEM((span, width), bf16),
        pltpu.VMEM((span, width), f32),
        pltpu.VMEM((span, 128), f32),
        pltpu.VMEM((span, width), bf16),
        pltpu.VMEM((s.panels, span, width), bf16),
        pltpu.VMEM((s.panels, span, width), bf16),
        pltpu.VMEM((span, width), f32),
        pltpu.VMEM((2, s.block, width), bf16),
        pltpu.VMEM((s.block, width), bf16),
        pltpu.VMEM((span, width), bf16),
        pltpu.VMEM((8, width), f32),
        pltpu.VMEM((3, 8, width), f32),
        pltpu.VMEM((3, 8, 128), f32),
        small,
        small,
        small,
        pltpu.VMEM((4, 8, 128), f32),
        pltpu.SemaphoreType.DMA((s.flying,)),
        pltpu.SemaphoreType.DMA((copies,)),
        pltpu.SemaphoreType.DMA((len(s.gather_blocks) + 2,)),
        pltpu.VMEM((both, 128), f32),
        pltpu.VMEM((4, 2, s.rows - s.out0, width), bf16),
        pltpu.VMEM((2, 4, s.rows - s.out0, width), bf16),
    ]
    return pl.pallas_call(
        functools.partial(layer_kernel, s),
        out_shape=[
            jax.ShapeDtypeStruct((span, width), bf16),
            jax.ShapeDtypeStruct((8, 128), f32),
            jax.ShapeDtypeStruct((span, width), f32),
            jax.ShapeDtypeStruct((s.out0, width), bf16),
            jax.ShapeDtypeStruct((s.up0 - s.out0, width), bf16),
            jax.ShapeDtypeStruct((s.shard, s.panels * width), bf16),
            jax.ShapeDtypeStruct((s.downs, width), bf16),
        ],
        in_specs=[anywhere, anywhere, vmem, smem, smem] + [anywhere] * 6,
        out_specs=[anywhere, vmem, anywhere] + [vmem] * 4,
        scratch_shapes=scratch,
        compiler_params=pltpu.CompilerParams(
            collective_id=0, has_side_effects=True, vmem_limit_bytes=s.vmem
        ),
    )(*args)


def fused_shards(
    tokens,
    w_query,
    w_key,
    w_value,
    w_out,
    w_up,
    w_down,
    gain_attn,
    gain_ffn,
    teacher,
    seq_lengths,
    tok_perm,
    valid_count,
):
    f32 = jnp.float32
    dp_count = lax.axis_size("dp")
    span, width = tokens.shape[1:]
    shard, ff = w_up.shape
    seq_len = tok_perm.shape[1]
    s = Sizes(span, width, ff, shard, w_down.shape[0], seq_len * dp_count)
    s.vmem = 63 * MIB
    gain_rows = jnp.pad(jnp.stack([gain_attn, gain_ffn]), ((0, 14), (0, width - shard)))
    ordered, total, token_grad, qkv, out, up, down = layer(
        s,
        tokens[0],
        teacher[0],
        tok_perm,
        seq_lengths,
        valid_count,
        w_query,
        w_key,
        w_value,
        jnp.concatenate([w_out, gain_rows]),
        w_up,
        w_down,
    )
    loss = (total[0, 0] / (2.0 * width * valid_count[0].astype(f32))).reshape(1)
    return (
        ordered[None],
        loss,
        token_grad[None],
        qkv[:shard].astype(f32),
        qkv[shard : 2 * shard].astype(f32),
        qkv[2 * shard :].astype(f32),
        out[:shard].astype(f32),
        up.astype(f32),
        down.astype(f32),
        out[shard, :shard].astype(f32),
        out[shard + 1, :shard].astype(f32),
    )


def solution(mesh):
    in_specs = (
        P("dp", "ctx", None),
        P("dp", None),
        P("dp", None),
        P("dp", None),
        P("dp", None),
        P("dp", None),
        P("dp", None),
        P("dp"),
        P("dp"),
        P("dp", "ctx", None),
        P("dp"),
        P("dp", None),
        P(),
    )
    out_specs = (
        P("dp", "ctx", None),
        P(),
        P("dp", "ctx", None),
        P("dp", None),
        P("dp", None),
        P("dp", None),
        P("dp", None),
        P("dp", None),
        P("dp", None),
        P("dp"),
        P("dp"),
    )
    body = fused_shards if dict(mesh.shape) == {"dp": 16, "ctx": 2} else shards
    return jax.shard_map(body, mesh=mesh, in_specs=in_specs, out_specs=out_specs, check_vma=False)
```

profile of v0, /device:TPU:0, one launch (start us, length us, event | category | flops | bytes accessed | tf_op | source)
XLA Modules:
  0.0 205.3 jit_solution(8232957324872759464)
XLA Ops:
  1.9 0.7 fusion.5
  2.6 1.5 pad_maximum_fusion.refs_8_
  4.2 190.1 %shard_map.212 = (bf16[512,768]{1,0:T(8,128)(2,1)}, f32[8,128]{1,0:T(8,128)}, f32[512,768]{1,0:T(8,128)}, bf16[144,768]{1,0:T(8,128)(2,1)}, bf16[64,768]{1,0:T(8...) custom-call(bf16[512,768]{1,0:T(8,128)(2,1)} %bitcast.17, bf16[512,768]{1,0:T(8,128)(2,1)} %bitcast.18, ...), custom_call_target="tpu_custom_call" | custom-call | tf_op jit(solution)/shard_map/pallas_call | solution.py:1278
  194.3 0.0 copy-start.2
  194.3 0.0 copy-start.1
  194.3 1.3 slice.21
  196.2 1.8 slice_convert_fusion.1
  198.0 0.0 copy-start
  198.0 1.9 convert_element_type.41
  200.0 0.0 copy-done.2
  200.0 0.9 convert_element_type.42
  200.8 1.3 bitcast_convert_fusion
  202.1 0.0 copy-done.1
  202.1 0.9 copy.28
  203.0 0.0 copy-done
  203.0 1.1 copy.29
Async XLA Ops:
  194.3 5.7 %copy-start.2 = (bf16[192,768]{1,0:T(8,128)(2,1)S(1)}, bf16[192,768]{1,0:T(8,128)(2,1)}, u32[]{:S(2)}) copy-start(bf16[192,768]{1,0:T(8,128)(2,1)} %get-tuple-element.24) | copy-start | bytes 884740
  194.3 7.8 %copy-start.1 = (bf16[512,768]{1,0:T(8,128)(2,1)S(1)}, bf16[512,768]{1,0:T(8,128)(2,1)}, u32[]{:S(2)}) copy-start(bf16[512,768]{1,0:T(8,128)(2,1)} %get-tuple-element.18) | copy-start | bytes 2359300
  198.0 4.9 %copy-start = (f32[512,768]{1,0:T(8,128)S(1)}, f32[512,768]{1,0:T(8,128)}, u32[]{:S(2)}) copy-start(f32[512,768]{1,0:T(8,128)} %get-tuple-element.20) | copy-start | bytes 4718596
where the time goes:
time: 206 us; the launch traced here: 205 us
  Pallas kernels  190 us (92%)
  other arithmetic  8.08 us (4%)
  between operations  3.76 us (2%)
  local copies, waits for them, and re-layouts  3.3 us (2%)
    pallas_call x1, Pallas kernels, layer(): pl.pallas_call(functools.partial(layer_kernel, s), out_shape=[jax.ShapeDt...  190 us

commit v1 on v0

--- a/solution.py
+++ b/solution.py
@@ -18,10 +18,10 @@
 MIB = 1024 * 1024
 
 
-GATHER_SPLIT = (1, 3, 5, 6, 7, 8, 9)
+GATHER_SPLIT = (0, 3, 5, 6, 7, 8, 10)
 REDUCE_SPLIT = (1, 2, 7, 8, 9, 11)
-EARLY = 4
-FORWARD = ((0, 1, 2, 3, 4, 5, 6, 7, 8, 9, 10), (), (0, 1, 0, 0, 2, 2, 3, 2, 1, 3, 4, 1, 5, 1), (), (3, 4, 6), (3,), (4, 5, 7), (6,), (8,), (5,), (5, 7), (), (), (6, 9), (), (6,), (), (8,), (), (), (7, 7), (10,), (9, 8, 8), (), (9, 10, 9), (), (10,), ())
+EARLY = 11
+FORWARD = ((0, 1, 2, 3, 4, 5, 6, 7, 8, 9, 10), (0,), (1, 2, 3, 4, 5, 6, 7, 8, 9, 10, 0, 1, 2, 3, 4, 5, 6, 7, 8, 9, 10, 0, 1, 2, 3, 4, 5, 6, 7, 8, 9, 0, 10, 1, 2, 1, 3, 2, 0, 4, 5, 0), (4, 6, 7, 8), (3, 9, 10), (3, 5), (9,), (5, 6), (6,), (7,), (7,), (), (), (8,), (), (), (), (8,), (), (), (), (10,), (), (), (), (10,), (), ())
 BACKWARD = ((0, 1), (0, 2), (3,), (1, 4), (2, 5), (3, 0, 6), (4, 5, 1, 0, 6, 7), (2, 7, 4), (), (3, 0, 1, 5, 8), (), (8, 4, 6), (2,), (), (5,), (7,), (1, 9), (3, 6, 10), (2, 8, 4, 9, 5, 10, 11), (2, 6, 7, 8, 11, 12), (3, 9, 12), (), (11, 8, 10, 7, 9, 3, 10, 11, 12, 8, 9, 11, 12, 10, 9, 10, 12, 12))
 
 
@@ -342,6 +342,10 @@
         self.z_up = [(self.z + k) % 4 for k in range(4)]
         self.z_down = [(self.z + 4 - k) % 4 for k in range(4)]
         self.to_z = [(self.z_up[k] * 4 + self.y * 2 + self.c, self.x) for k in range(4)]
+        z = self.z
+        self.above = [(jnp.logical_and(z >= d, z < 3), z > d) for d in range(3)]
+        self.below = [(jnp.logical_and(z <= 3 - d, z > 0), z < 3 - d) for d in range(3)]
+        self.to_above, self.to_below = self.to_z[1], self.to_z[3]
 
     def barrier(self):
         semaphore = pltpu.get_barrier_semaphore()
@@ -351,9 +355,9 @@
 
 
 class Copy:
-    def __init__(self, refs, send, at, recv, to, partner):
+    def __init__(self, refs, send, at, recv, to, partner, when):
         self.refs, self.send, self.at, self.recv, self.to = refs, send, at, recv, to
-        self.partner = partner
+        self.partner, self.when = partner, when
 
     def make(self):
         src, dst = self.refs()
@@ -366,11 +370,20 @@
             device_id_type=MESH,
         )
 
+    def only(self, side, action):
+        if self.when is None:
+            action()
+        else:
+            pl.when(self.when[side])(action)
+
+    def start(self):
+        self.only(0, lambda: self.make().start())
+
     def wait_send(self):
-        self.make().wait_send()
+        self.only(0, lambda: self.make().wait_send())
 
     def wait_recv(self):
-        self.make().wait_recv()
+        self.only(1, lambda: self.make().wait_recv())
 
 
 class Links:
@@ -378,13 +391,13 @@
         self.send, self.recv, self.used, self.flying = send, recv, 0, []
         self.free = list(range(send.shape[0]))
 
-    def start(self, refs, partner):
+    def start(self, refs, partner, when=None):
         if not self.free:
             self.sent(self.flying[0][0])
         at = self.free.pop(0)
-        copy = Copy(refs, self.send, at, self.recv, self.used, partner)
+        copy = Copy(refs, self.send, at, self.recv, self.used, partner, when)
         self.used += 1
-        copy.make().start()
+        copy.start()
         self.flying.append((copy, at))
         return copy
 
@@ -410,7 +423,7 @@
         self.own_sem = own_sem
         self.mine, self.theirs = self.half(place.x), self.half(place.xo)
         self.source = self.half(place.x, shift)
-        self.last = 4 if self.split else 3
+        self.last = 6 if self.split else 5
 
     def cols(self, shift=0):
         return pl.ds(self.col0 + shift, self.width)
@@ -430,40 +443,52 @@
             self.shard.at[:, self.cols(self.shift)], self.piece(p.z, p.y, self.cols()), self.own_sem()
         )
 
-    def push(self, z, y, cols, partner):
-        return self.links.start(lambda: (self.piece(z, y, cols),) * 2, partner)
-
-    def send_own(self, partner):
+    def push(self, z, y, cols, partner, when=None):
+        return self.links.start(lambda: (self.piece(z, y, cols),) * 2, partner, when)
+
+    def send_own(self, partner, when=None):
         p = self.p
         return self.links.start(
-            lambda: (self.shard.at[:, self.source], self.piece(p.z, p.y, self.mine)), partner
+            lambda: (self.shard.at[:, self.source], self.piece(p.z, p.y, self.mine)), partner, when
         )
 
     def step0(self):
         p = self.p
-        self.from_z = [self.send_own(p.to_z[k]) for k in range(1, 4)]
+        self.up, self.down = self.send_own(p.to_above, p.above[0]), self.send_own(p.to_below, p.below[0])
         self.own().start()
+        self.from_x, self.from_y = [], []
         if self.early:
-            self.own_y()
-
-    def own_y(self):
-        self.from_y = [self.send_own(self.p.to_y)]
+            self.from_y.append(self.send_own(p.to_y))
+
+    def hop(self, d):
+        p = self.p
+        up, down = self.up, self.down
+        up.wait_recv()
+        if d < 2:
+            self.up = self.push(p.z_down[d + 1], p.y, self.mine, p.to_above, p.above[d + 1])
+        down.wait_recv()
+        if d < 2:
+            self.down = self.push(p.z_up[d + 1], p.y, self.mine, p.to_below, p.below[d + 1])
+        for z, there in ((p.z_down[d + 1], p.above[d][1]), (p.z_up[d + 1], p.below[d][1])):
+            when = (there, there)
+            self.from_y.append(self.push(z, p.y, self.mine, p.to_y, when))
+            if self.split:
+                self.from_x.append(self.push(z, p.y, self.mine, p.to_x, when))
 
     def step1(self):
-        p = self.p
         if not self.early:
-            self.own_y()
-        self.from_x = []
-        for k in range(1, 4):
-            self.from_z[k - 1].wait_recv()
-            piece = (p.z_down[k], p.y, self.mine)
-            self.from_y.append(self.push(*piece, p.to_y))
-            if self.split:
-                self.from_x.append(self.push(*piece, p.to_x))
+            self.from_y.append(self.send_own(self.p.to_y))
+        self.hop(0)
+
+    def step2(self):
+        self.hop(1)
+
+    def step3(self):
+        self.hop(2)
         self.own().wait()
-        self.from_c = [self.push(slice(None), p.y, self.mine, p.to_c)]
-
-    def step2(self):
+        self.from_c = [self.push(slice(None), self.p.y, self.mine, self.p.to_c)]
+
+    def step4(self):
         p, every = self.p, slice(None)
         for copy in self.from_y:
             copy.wait_recv()
@@ -475,14 +500,14 @@
                 copy.wait_recv()
             self.from_c.append(self.push(every, p.y, self.theirs, p.to_c))
 
-    def step3(self):
+    def step5(self):
         if self.split:
             self.across.wait_recv()
             self.from_c.append(self.push(slice(None), self.p.yo, self.theirs, self.p.to_c))
         else:
-            self.step4()
-
-    def step4(self):
+            self.step6()
+
+    def step6(self):
         for copy in self.from_c:
             copy.wait_recv()
 
@@ -748,7 +773,7 @@
 
 def layer_kernel(s, *refs):
     tokens, teacher, order_row, length, valid = refs[:5]
-    weights, (ordered_out, total_out, token_out), outs = refs[5:11], refs[11:14], refs[14:18]
+    weights, (ordered_out, loss_out, token_out), outs = refs[5:11], refs[11:14], refs[14:18]
     refs = refs[8:]
     (W, G, tok, QKV, dO, stat, attn, n1, r1, low1, act, gp, acc, teach, res_in, low2, gains, sums) = refs[10:28]
     total_refs, (send, recv, local), (order_col, core_in, bufs) = refs[28:33], refs[33:36], refs[36:]
@@ -1198,7 +1223,7 @@
     beat()
     beat()
     assert all(item.stage > item.last for item in reduces)
-    total_out[...] = total.sum()
+    loss_out[0] = jnp.max(total.sum() / (2.0 * width * valid_total))
     token_copy.wait()
     ordered_copy.wait()
     links.drain()
@@ -1241,7 +1266,7 @@
     vmem = pl.BlockSpec(memory_space=pltpu.VMEM)
     smem = pl.BlockSpec(memory_space=pltpu.SMEM)
     back = s.down_blocks + s.up_blocks + [s.out_block] + s.last_blocks
-    copies = sum(15 if b[2] else 9 for b in s.gather_blocks)
+    copies = sum(24 if b[2] else 15 for b in s.gather_blocks)
     copies += sum(8 if b[2] else 6 for b in back) + 6 + 5
     small = pltpu.VMEM((8, 128), f32)
     scratch = [
@@ -1279,7 +1304,7 @@
         functools.partial(layer_kernel, s),
         out_shape=[
             jax.ShapeDtypeStruct((span, width), bf16),
-            jax.ShapeDtypeStruct((8, 128), f32),
+            jax.ShapeDtypeStruct((1,), f32),
             jax.ShapeDtypeStruct((span, width), f32),
             jax.ShapeDtypeStruct((s.out0, width), bf16),
             jax.ShapeDtypeStruct((s.up0 - s.out0, width), bf16),
@@ -1287,7 +1312,7 @@
             jax.ShapeDtypeStruct((s.downs, width), bf16),
         ],
         in_specs=[anywhere, anywhere, vmem, smem, smem] + [anywhere] * 6,
-        out_specs=[anywhere, vmem, anywhere] + [vmem] * 4,
+        out_specs=[anywhere, smem, anywhere] + [vmem] * 4,
         scratch_shapes=scratch,
         compiler_params=pltpu.CompilerParams(
             collective_id=0, has_side_effects=True, vmem_limit_bytes=s.vmem
@@ -1318,7 +1343,7 @@
     s = Sizes(span, width, ff, shard, w_down.shape[0], seq_len * dp_count)
     s.vmem = 63 * MIB
     gain_rows = jnp.pad(jnp.stack([gain_attn, gain_ffn]), ((0, 14), (0, width - shard)))
-    ordered, total, token_grad, qkv, out, up, down = layer(
+    ordered, loss, token_grad, qkv, out, up, down = layer(
         s,
         tokens[0],
         teacher[0],
@@ -1332,7 +1357,6 @@
         w_up,
         w_down,
     )
-    loss = (total[0, 0] / (2.0 * width * valid_count[0].astype(f32))).reshape(1)
     return (
         ordered[None],
         loss,

time: 206 us -> 201 us (0.976)
  Pallas kernels: 190 us -> 187 us
    pallas_call x1, Pallas kernels: 190 us -> 187 us  [layer(): pl.pallas_call(functools.partial(layer_kernel, s), out_shape=[jax.ShapeDt...]
where the time goes in v1:
time: 201 us
  Pallas kernels  187 us (93%)
  other arithmetic  8.1 us (4%)
  between operations  3.73 us (2%)
  local copies, waits for them, and re-layouts  2.04 us (1%)
    pallas_call x1, Pallas kernels, layer(): pl.pallas_call(functools.partial(layer_kernel, s), out_shape=[jax.ShapeDt...  187 us

profile of v1, /device:TPU:0, one launch (start us, length us, event | category | flops | bytes accessed | tf_op | source)
XLA Modules:
  0.0 201.1 jit_solution(10231552503991737042)
XLA Ops:
  1.9 0.7 fusion.5
  2.6 1.5 pad_maximum_fusion.refs_8_
  4.2 187.2 %shard_map.212 = (bf16[512,768]{1,0:T(8,128)(2,1)}, f32[1]{0:T(128)}, f32[512,768]{1,0:T(8,128)}, bf16[144,768]{1,0:T(8,128)(2,1)}, bf16[64,768]{1,0:T(8,128)(2,...) custom-call(bf16[512,768]{1,0:T(8,128)(2,1)} %bitcast.14, bf16[512,768]{1,0:T(8,128)(2,1)} %bitcast.15, ...), custom_call_target="tpu_custom_call" | custom-call | tf_op jit(solution)/shard_map/pallas_call | solution.py:1303
  191.3 0.0 copy-start.2
  191.4 0.0 copy-start.1
  191.4 1.3 bitcast_convert_fusion
  192.7 1.8 slice_convert_fusion.1
  194.5 0.0 copy-start
  194.5 1.9 convert_element_type.36
  196.4 0.0 copy-done.2
  196.4 0.9 convert_element_type.37
  197.3 0.0 copy-done.1
  197.3 0.9 copy.29
  198.8 0.0 copy-done
  198.8 1.1 copy.31
Async XLA Ops:
  191.3 5.1 %copy-start.2 = (bf16[192,768]{1,0:T(8,128)(2,1)S(1)}, bf16[192,768]{1,0:T(8,128)(2,1)}, u32[]{:S(2)}) copy-start(bf16[192,768]{1,0:T(8,128)(2,1)} %get-tuple-element.24) | copy-start | bytes 884740
  191.4 5.9 %copy-start.1 = (bf16[512,768]{1,0:T(8,128)(2,1)S(1)}, bf16[512,768]{1,0:T(8,128)(2,1)}, u32[]{:S(2)}) copy-start(bf16[512,768]{1,0:T(8,128)(2,1)} %get-tuple-element.18) | copy-start | bytes 2359300
  194.5 4.3 %copy-start = (f32[512,768]{1,0:T(8,128)S(1)}, f32[512,768]{1,0:T(8,128)}, u32[]{:S(2)}) copy-start(f32[512,768]{1,0:T(8,128)} %get-tuple-element.20) | copy-start | bytes 4718596

commit v2 on v1

--- a/solution.py
+++ b/solution.py
@@ -521,7 +521,7 @@
         self.grads, self.out = grads, out
         self.p, self.links = place, links
         self.core_in, self.bufs = core_in, bufs
-        limit = 32 * 768 // self.width
+        limit = 96 * 768 // self.width
         self.block = max(b for b in range(16, min(self.rows, limit) + 1, 16) if self.rows % b == 0)
         self.stage = 0
         self.mine, self.theirs = self.half(place.x), self.half(place.xo)
@@ -550,9 +550,7 @@
             first = pl.multiple_of((i % steps) * self.block, 16)
             put = target(i // steps, pl.ds(self.at0 + first, self.block))
             given = source(i // steps, pl.ds(self.here0 + first, self.block))
-            self.grads[put] = (
-                self.grads[put].astype(jnp.float32) + given.astype(jnp.float32)
-            ).astype(jnp.bfloat16)
+            self.grads[put] = self.grads[put] + given
             return carry
 
         lax.fori_loop(0, outer * steps, body, 0)
@@ -1255,7 +1253,7 @@
         self.down_blocks, self.up_blocks = back[:3], back[3:-5]
         self.out_block, self.last_blocks = back[-5], back[-4:]
         self.forward, self.backward = FORWARD, BACKWARD
-        self.rows_n, self.flying = 64, 64
+        self.rows_n, self.flying = 256, 128
 
 
 def layer(s, *args):

time: 201 us -> 196 us (0.975)
  Pallas kernels: 187 us -> 181 us
    pallas_call x1, Pallas kernels: 187 us -> 181 us  [layer(): pl.pallas_call(functools.partial(layer_kernel, s), out_shape=[jax.ShapeDt...]
where the time goes in v2:
time: 196 us; the launch traced here: 195 us
  Pallas kernels  181 us (92%)
  other arithmetic  8.1 us (4%)
  between operations  3.73 us (2%)
  local copies, waits for them, and re-layouts  2.04 us (1%)
    pallas_call x1, Pallas kernels, layer(): pl.pallas_call(functools.partial(layer_kernel, s), out_shape=[jax.ShapeDt...  181 us

profile of v2, /device:TPU:0, one launch (start us, length us, event | category | flops | bytes accessed | tf_op | source)
XLA Modules:
  0.0 195.2 jit_solution(5991899176254661578)
XLA Ops:
  1.9 0.7 fusion.5
  2.6 1.5 pad_maximum_fusion.refs_8_
  4.2 181.4 %shard_map.212 = (bf16[512,768]{1,0:T(8,128)(2,1)}, f32[1]{0:T(128)}, f32[512,768]{1,0:T(8,128)}, bf16[144,768]{1,0:T(8,128)(2,1)}, bf16[64,768]{1,0:T(8,128)(2,...) custom-call(bf16[512,768]{1,0:T(8,128)(2,1)} %bitcast.14, bf16[512,768]{1,0:T(8,128)(2,1)} %bitcast.15, ...), custom_call_target="tpu_custom_call" | custom-call | tf_op jit(solution)/shard_map/pallas_call | solution.py:1301
  185.5 0.0 copy-start.2
  185.5 0.0 copy-start.1
  185.6 1.3 bitcast_convert_fusion
  186.8 1.8 slice_convert_fusion.1
  188.7 0.0 copy-start
  188.7 1.9 convert_element_type.36
  190.6 0.0 copy-done.2
  190.6 0.9 convert_element_type.37
  191.4 0.0 copy-done.1
  191.5 0.9 copy.29
  193.0 0.0 copy-done
  193.0 1.1 copy.31
Async XLA Ops:
  185.5 5.1 %copy-start.2 = (bf16[192,768]{1,0:T(8,128)(2,1)S(1)}, bf16[192,768]{1,0:T(8,128)(2,1)}, u32[]{:S(2)}) copy-start(bf16[192,768]{1,0:T(8,128)(2,1)} %get-tuple-element.24) | copy-start | bytes 884740
  185.5 5.9 %copy-start.1 = (bf16[512,768]{1,0:T(8,128)(2,1)S(1)}, bf16[512,768]{1,0:T(8,128)(2,1)}, u32[]{:S(2)}) copy-start(bf16[512,768]{1,0:T(8,128)(2,1)} %get-tuple-element.18) | copy-start | bytes 2359300
  188.7 4.3 %copy-start = (f32[512,768]{1,0:T(8,128)S(1)}, f32[512,768]{1,0:T(8,128)}, u32[]{:S(2)}) copy-start(f32[512,768]{1,0:T(8,128)} %get-tuple-element.20) | copy-start | bytes 4718596

commit v3 on v2

--- a/solution.py
+++ b/solution.py
@@ -845,9 +845,8 @@
     own_teacher.wait()
     for n in range(3):
         cols = slice(n * third, (n + 1) * third)
-        gp[1, : s.block, cols] = dot(pick(xo), gp[0, :, cols]).astype(bf16)
+        low2[: s.block, cols] = dot(pick(xo), gp[0, :, cols]).astype(bf16)
         teach[x, :, cols] = dot(pick(x), gp[0, :, cols]).astype(bf16)
-    teach_copy = links.start(lambda: (gp.at[1, pl.ds(0, s.block)], teach.at[x]), place.to_x)
     advance()
     arrived(0, 1, 2)
 
@@ -896,6 +895,7 @@
         each(pair, pairs, advance)
 
     loop(pairs, attend)
+    teach_copy = links.start(lambda: (low2.at[pl.ds(0, s.block)], teach.at[x]), place.to_x)
 
     arrived(3)
     device = lax.broadcasted_iota(jnp.int32, (16, width), 0)
@@ -933,8 +933,6 @@
     loop(span // rows_n, first_norm)
     advance()
 
-    teach_copy.wait_recv()
-    links.sent(teach_copy)
 
     def ahead(i, count):
         steps = iter(range(count))
@@ -971,6 +969,8 @@
     advance()
     assert all(stage > item.last for stage, item in zip(stages, gathers))
 
+    teach_copy.wait_recv()
+    links.sent(teach_copy)
     sums[...] = jnp.zeros_like(sums)
     valid_total = jnp.full((1, 1), valid[0], jnp.int32).astype(f32)
     grad_scale = s.tokens / valid_total

time: 196 us -> 196 us (level)
  no operation moved by 1% of the time
where the time goes in v3:
time: 196 us; the launch traced here: 195 us
  Pallas kernels  182 us (93%)
  other arithmetic  8.1 us (4%)
  between operations  3.73 us (2%)
  local copies, waits for them, and re-layouts  2.04 us (1%)
    pallas_call x1, Pallas kernels, layer(): pl.pallas_call(functools.partial(layer_kernel, s), out_shape=[jax.ShapeDt...  182 us

profile of v3, /device:TPU:0, one launch (start us, length us, event | category | flops | bytes accessed | tf_op | source)
XLA Modules:
  0.0 195.4 jit_solution(2684858964658677562)
XLA Ops:
  1.9 0.7 fusion.5
  2.6 1.5 pad_maximum_fusion.refs_8_
  4.2 181.5 %shard_map.212 = (bf16[512,768]{1,0:T(8,128)(2,1)}, f32[1]{0:T(128)}, f32[512,768]{1,0:T(8,128)}, bf16[144,768]{1,0:T(8,128)(2,1)}, bf16[64,768]{1,0:T(8,128)(2,...) custom-call(bf16[512,768]{1,0:T(8,128)(2,1)} %bitcast.14, bf16[512,768]{1,0:T(8,128)(2,1)} %bitcast.15, ...), custom_call_target="tpu_custom_call" | custom-call | tf_op jit(solution)/shard_map/pallas_call | solution.py:1301
  185.7 0.0 copy-start.2
  185.7 0.0 copy-start.1
  185.7 1.3 bitcast_convert_fusion
  187.0 1.8 slice_convert_fusion.1
  188.8 0.0 copy-start
  188.8 1.9 convert_element_type.36
  190.7 0.0 copy-done.2
  190.7 0.9 convert_element_type.37
  191.6 0.0 copy-done.1
  191.6 0.9 copy.29
  193.1 0.0 copy-done
  193.1 1.1 copy.31
Async XLA Ops:
  185.7 5.1 %copy-start.2 = (bf16[192,768]{1,0:T(8,128)(2,1)S(1)}, bf16[192,768]{1,0:T(8,128)(2,1)}, u32[]{:S(2)}) copy-start(bf16[192,768]{1,0:T(8,128)(2,1)} %get-tuple-element.24) | copy-start | bytes 884740
  185.7 5.9 %copy-start.1 = (bf16[512,768]{1,0:T(8,128)(2,1)S(1)}, bf16[512,768]{1,0:T(8,128)(2,1)}, u32[]{:S(2)}) copy-start(bf16[512,768]{1,0:T(8,128)(2,1)} %get-tuple-element.18) | copy-start | bytes 2359300
  188.8 4.3 %copy-start = (f32[512,768]{1,0:T(8,128)S(1)}, f32[512,768]{1,0:T(8,128)}, u32[]{:S(2)}) copy-start(f32[512,768]{1,0:T(8,128)} %get-tuple-element.20) | copy-start | bytes 4718596
